TPU v7x, 32 devices: a whole 2x2x4 slice. The times are simulated.
32 devices in a mesh: row: 4 (over z), col: 2 (over x), depth: 4 (over y, core).
Axes of the slice: x: 2, y: 2, z: 4, core: 2. Of those that a mesh axis runs over, the one named last changes fastest.
Arguments:
- grad_out: bfloat16 [2048, 3072], P(('row', 'depth'), 'col'), may hold values from -4 to 4
- input_stash: bfloat16 [2048, 3072], P(('row', 'depth'), 'col'), may hold values from -6 to 6
- input_scale: float32 [24, 2048], P('col', ('row', 'depth')), may hold values from 0.05 to 0.8
- hidden_stash: bfloat16 [2048, 12288], P(('row', 'depth'), 'col'), may hold values from -6 to 6
- hidden_scale: float32 [96, 2048], P('col', ('row', 'depth')), may hold values from 0.25 to 4
- first_weight: bfloat16 [3072, 12288], P('col', 'row'), may hold values from -0.0546875 to 0.0546875
- second_weight: bfloat16 [12288, 3072], P('col', 'row'), may hold values from -0.109375 to 0.109375
Outputs:
- input_grad: bfloat16 [2048, 3072], P(('row', 'depth'), 'col')
- first_grad: bfloat16 [3072, 12288], P('col', ('row', 'depth'))
- first_bias: float32 [12288], P(('row', 'depth'))
- second_grad: bfloat16 [12288, 3072], P('col', ('row', 'depth'))
- second_bias: float32 [3072], P(('row', 'depth'))
All inputs are finite; a program needn't handle non-finite values.
Results may differ from a plain program's by a relative error of at most 0.015.
Values may be sent and summed in bfloat16 or wider, within the bound.
No kernel may reach another device: no remote copies, remote signals or barrier semaphores. Data moves between devices by JAX's collectives and lax.ppermute only.
A program may use at most 192 MiB of HBM per device.

v0:
```python
import jax
import jax.numpy as jnp
from jax import lax
from jax.sharding import PartitionSpec as P

root_two_over_pi = 0.7978845608028654
cubic_coef = 0.044715
contract_last = (((1,), (1,)), ((), ()))
contract_first = (((0,), (0,)), ((), ()))


def dequantize(values, scales):
    height = values.shape[0]
    breadth = values.shape[1]
    block = breadth // scales.shape[0]
    blocks = values.astype(jnp.float32).reshape(height, breadth // block, block)
    return (blocks * jnp.transpose(scales)[:, :, None]).reshape(height, breadth)


def gelu_value(before):
    tangent = jnp.tanh(root_two_over_pi * (before + cubic_coef * before * before * before))
    return 0.5 * before * (1.0 + tangent)


def gelu_slope(before):
    tangent = jnp.tanh(root_two_over_pi * (before + cubic_coef * before * before * before))
    return 0.5 * (1.0 + tangent) + 0.5 * before * (1.0 - tangent * tangent) * root_two_over_pi * (
        1.0 + 3.0 * cubic_coef * before * before
    )


def per_device(
    grad_out, input_stash, input_scale, hidden_stash, hidden_scale, first_weight, second_weight
):
    full_grad = lax.all_gather(grad_out, "col", axis=1, tiled=True)
    grad_rows = lax.all_to_all(full_grad, "row", split_axis=1, concat_axis=0, tiled=True)
    columns = full_grad
    hidden_grad = lax.dot_general(
        columns,
        lax.all_gather(second_weight, "row", axis=1, tiled=True),
        contract_last,
        preferred_element_type=jnp.float32,
    )
    before_gelu = dequantize(hidden_stash, hidden_scale)
    gelu_grad = (hidden_grad * gelu_slope(before_gelu)).astype(jnp.bfloat16)
    full_gelu = lax.all_gather(gelu_grad, "col", axis=1, tiled=True)
    gelu_rows = lax.all_to_all(full_gelu, "row", split_axis=1, concat_axis=0, tiled=True)
    columns = full_gelu
    input_sum = lax.dot_general(
        columns,
        lax.all_gather(first_weight, "row", axis=1, tiled=True),
        contract_last,
        preferred_element_type=jnp.float32,
    )
    input_grad = input_sum.astype(jnp.bfloat16)
    stash_rows, scale_rows = (
        lax.all_gather(input_stash, "row", axis=0, tiled=True),
        lax.all_gather(input_scale.astype(jnp.bfloat16), "row", axis=1, tiled=True).astype(
            input_scale.dtype
        ),
    )
    inputs = dequantize(stash_rows, scale_rows).astype(jnp.bfloat16)
    hidden_values, hidden_scales = (
        lax.all_gather(hidden_stash, "row", axis=0, tiled=True),
        lax.all_gather(hidden_scale.astype(jnp.bfloat16), "row", axis=1, tiled=True).astype(
            hidden_scale.dtype
        ),
    )
    hidden = gelu_value(dequantize(hidden_values, hidden_scales)).astype(jnp.bfloat16)
    first_term = lax.dot_general(
        inputs, gelu_rows, contract_first, preferred_element_type=jnp.float32
    )
    first_column = jnp.sum(gelu_rows.astype(jnp.float32), axis=0)
    first_grad, first_bias = (
        lax.psum_scatter(
            first_term.astype(jnp.bfloat16), "depth", scatter_dimension=1, tiled=True
        ).astype(jnp.float32),
        lax.psum_scatter(
            first_column.astype(jnp.bfloat16), "depth", scatter_dimension=0, tiled=True
        ).astype(jnp.float32),
    )
    second_term = lax.dot_general(
        hidden, grad_rows, contract_first, preferred_element_type=jnp.float32
    )
    second_column = jnp.sum(grad_rows.astype(jnp.float32), axis=0)
    second_grad, second_bias = (
        lax.psum_scatter(
            second_term.astype(jnp.bfloat16), "depth", scatter_dimension=1, tiled=True
        ).astype(jnp.float32),
        lax.psum_scatter(
            second_column.astype(jnp.bfloat16), "depth", scatter_dimension=0, tiled=True
        ).astype(jnp.float32),
    )
    return (
        input_grad,
        first_grad.astype(jnp.bfloat16),
        first_bias,
        second_grad.astype(jnp.bfloat16),
        second_bias,
    )


def solution(mesh):
    placed = (
        P(("row", "depth"), "col"),
        P(("row", "depth"), "col"),
        P("col", ("row", "depth")),
        P(("row", "depth"), "col"),
        P("col", ("row", "depth")),
        P("col", "row"),
        P("col", "row"),
    )
    return jax.shard_map(
        per_device,
        mesh=mesh,
        in_specs=placed,
        out_specs=(
            P(("row", "depth"), "col"),
            P("col", ("row", "depth")),
            P(("row", "depth")),
            P("col", ("row", "depth")),
            P(("row", "depth")),
        ),
        check_vma=False,
    )
```

profile of v0, /device:TPU:0, one launch (start us, length us, event | category | flops | bytes accessed | tf_op | source)
XLA Modules:
  0.0 1713.9 jit_solution(17803450040426796435)
XLA Ops:
  7.2 0.0 copy-start.3
  7.2 0.0 copy-start.5
  7.2 0.0 all-gather.6.cloned.1.call-start
  7.2 0.7 all-gather.6.cloned.1.call-update
  7.9 0.0 all-gather.14.cloned.1.call-start
  8.0 0.7 all-gather.14.cloned.1.call-update
  8.7 0.0 all-gather.8.cloned.1.call-start
  8.7 0.0 copy-done.3
  8.7 0.2 copy.25
  9.0 0.0 copy-done.5
  9.0 0.1 copy.26
  9.1 12.8 all_gather.24
  21.9 621.9 %all-gather.6.cloned.1.call-done = bf16[6144,3072]{1,0:T(8,128)(2,1)} async-done(((bf16[6144,768]{1,0:T(8,128)(2,1)}), bf16[6144,3072]{1,0:T(8,128)(2,1)}) %all-gather.6.cloned.1.call-update) | async-done | bytes 37748752 | tf_op jit(solution)/shard_map/all_gather | solution.py:40
  643.8 0.9 mul.105
  644.7 0.0 copy-start.4
  644.7 20.3 %fusion.5 = bf16[128,6144]{1,0:T(8,128)(2,1)} fusion(bf16[128,3072]{0,1:T(8,128)(2,1)} %all_gather.24, bf16[6144,3072]{1,0:T(8,128)(2,1)} %all-gather.6.cloned.1.call-done, f32[16,8,48,128]{3,2,1,0:T(8,128)S(1)} %bitcast.43, bf16[128,6144]{1,0:T(8,128)(2,1)} %param.10), kind=kOutput, calls=%fused_computation.10 | convolution fusion | flops 4848353280 | bytes 44826624 | tf_op jit(solution)/shard_map/dot_general | solution.py:38
  665.0 0.0 all-gather.8.cloned.1.call-update
  665.0 0.0 all-gather.12.cloned.1.call-start
  665.1 0.0 copy-done.4
  665.1 0.9 copy.27
  666.0 0.0 all-gather.12.cloned.1.call-update
  666.0 0.0 copy-start.6
  666.0 0.0 all-gather.10.cloned.1.call-start
  666.1 0.5 all-gather.10.cloned.1.call-update
  666.6 3.5 all-to-all-start.1
  670.1 0.0 reduce-scatter.5.cloned.1.call-start
  670.2 0.0 copy-done.6
  670.2 53.5 %all_gather.31 = bf16[48,512]{1,0:T(8,128)(2,1)S(1)} all-gather(bf16[48,128]{1,0:T(8,128)(2,1)S(1)} %convert_element_type.58), channel_id=1, replica_groups=mesh['row'=4,'col'=2,'depth'=4] {'row'}, dimensions={1}, use_global_device_ids=true | all-gather | bytes 61440 | tf_op jit(solution)/shard_map/all_gather | solution.py:65
  723.8 0.1 copy.29
  723.9 0.0 all-to-all-done.1
  723.9 0.0 copy-start.2
  723.9 1.2 copy.30
  725.1 51.7 %all-gather.14.cloned.1.call-done = bf16[512,6144]{1,0:T(8,128)(2,1)} async-done(((bf16[128,6144]{1,0:T(8,128)(2,1)}), bf16[512,6144]{1,0:T(8,128)(2,1)}) %all-gather.14.cloned.1.call-update) | async-done | bytes 6291472 | tf_op jit(solution)/shard_map/all_gather | solution.py:64
  776.8 0.0 copy-done.2
  776.8 3.4 mul.126
  780.2 14.7 convolution_convert_fusion.1
  795.0 0.0 reduce-scatter.5.cloned.1.call-update
  795.0 27.0 %all-gather.8.cloned.1.call-done = bf16[128,12288]{1,0:T(8,128)(2,1)} async-done(((bf16[128,6144]{1,0:T(8,128)(2,1)}), bf16[128,12288]{1,0:T(8,128)(2,1)}) %all-gather.8.cloned.1.call-update) | async-done | bytes 3145744 | tf_op jit(solution)/shard_map/all_gather | solution.py:46
  822.0 3.8 copy.42
  825.8 4.7 all-to-all-start
  830.5 0.0 reduce-scatter.3.cloned.1.call-start
  830.5 0.0 copy-done.7
  830.5 101.3 %all_gather.29 = bf16[12,512]{1,0:T(8,128)(2,1)S(1)} all-gather(bf16[12,128]{1,0:T(8,128)(2,1)S(1)} %convert_element_type.53), channel_id=1, replica_groups=mesh['row'=4,'col'=2,'depth'=4] {'row'}, dimensions={1}, use_global_device_ids=true | all-gather | bytes 15360 | tf_op jit(solution)/shard_map/all_gather | solution.py:58
  931.8 0.0 all-gather.12.cloned.1.call-done
  931.8 3.2 fusion.16
  935.0 0.0 all-to-all-done
  935.0 0.0 copy-start.1
  935.0 10.3 convolution_convert_fusion
  945.2 0.0 copy-done.1
  945.2 0.0 copy-start.8
  945.2 0.0 copy-start
  945.2 0.0 reduce-scatter.3.cloned.1.call-update
  945.3 0.6 copy-done.8
  945.9 0.6 dynamic-slice
  947.8 1.3 reduce_sum.25
  949.1 596.2 %all-gather.10.cloned.1.call-done = bf16[1536,12288]{1,0:T(8,128)(2,1)} async-done(((bf16[1536,3072]{1,0:T(8,128)(2,1)}), bf16[1536,12288]{1,0:T(8,128)(2,1)}) %all-gather.10.cloned.1.call-update) | async-done | bytes 37748752 | tf_op jit(solution)/shard_map/all_gather | solution.py:51
  1545.4 0.0 copy-done
  1545.4 21.6 %convolution_convert_fusion.2 = bf16[128,1536]{1,0:T(8,128)(2,1)} fusion(bf16[128,12288]{1,0:T(8,128)(2,1)S(1)} %copy-done, bf16[1536,12288]{1,0:T(8,128)(2,1)} %all-gather.10.cloned.1.call-done), kind=kOutput, calls=%fused_computation.26 | convolution fusion | flops 4832034816 | bytes 41287680 | tf_op jit(solution)/shard_map/dot_general | solution.py:49
  1567.0 2.5 reduce_sum.24
  1569.6 6.8 all-reduce.2
  1576.4 0.6 dynamic-slice_convert_fusion.1
  1577.0 0.7 dynamic-slice_convert_fusion
  1577.7 48.0 %reduce-scatter.5.cloned.1.call-done = bf16[6144,192]{0,1:T(8,128)(2,1)} async-done(((bf16[6144,768]{0,1:T(8,128)(2,1)}), bf16[6144,192]{0,1:T(8,128)(2,1)}) %reduce-scatter.5.cloned.1.call-update) | async-done | bytes 2359312 | tf_op jit(solution)/shard_map/reduce_scatter | solution.py:87
  1625.7 81.4 %reduce-scatter.3.cloned.1.call-done = bf16[1536,768]{1,0:T(8,128)(2,1)} async-done(((bf16[1536,3072]{1,0:T(8,128)(2,1)}), bf16[1536,768]{1,0:T(8,128)(2,1)}) %reduce-scatter.3.cloned.1.call-update) | async-done | bytes 2359312 | tf_op jit(solution)/shard_map/reduce_scatter | solution.py:75
  (5 shorter events, 0.0 us)
Async XLA Ops:
  7.2 1.6 copy-start.3
  7.2 1.8 copy-start.5
  7.2 636.6 %all-gather.6.cloned.1.call-start = ((), (), s32[]{:S(2)}) async-start(), calls=%async_computation.4 | async-start | bytes 47185920 | tf_op jit(solution)/shard_map/all_gather | solution.py:40
  7.9 768.9 %all-gather.14.cloned.1.call-start = ((), (), s32[]{:S(2)}) async-start(), calls=%async_computation.9 | async-start | bytes 7864320 | tf_op jit(solution)/shard_map/all_gather | solution.py:64
  8.7 813.3 %all-gather.8.cloned.1.call-start = ((), (), s32[]{:S(2)}) async-start(), calls=%async_computation.5 | async-start | bytes 4718592 | tf_op jit(solution)/shard_map/all_gather | solution.py:46
  644.7 20.4 %copy-start.4 = (bf16[128,1536]{1,0:T(8,128)(2,1)S(1)}, bf16[128,1536]{1,0:T(8,128)(2,1)}, u32[]{:S(2)}) copy-start(bf16[128,1536]{1,0:T(8,128)(2,1)} %param.8) | copy-start | bytes 1179652
  665.0 266.8 %all-gather.12.cloned.1.call-start = ((), (), s32[]{:S(2)}) async-start(), calls=%async_computation.7 | async-start | bytes 1966080 | tf_op jit(solution)/shard_map/all_gather | solution.py:57
  666.0 4.2 copy-start.6
  666.0 879.3 %all-gather.10.cloned.1.call-start = ((), (), s32[]{:S(2)}) async-start(), calls=%async_computation.6 | async-start | bytes 47185920 | tf_op jit(solution)/shard_map/all_gather | solution.py:51
  666.6 57.3 %all-to-all-start.1 = ((bf16[128,4,768]{0,2,1:T(8,128)(2,1)}), bf16[128,4,768]{0,2,1:T(8,128)(2,1)S(1)}, u32[]{:S(2)}, u32[]{:S(2)}) async-start(bf16[128,4,768]{0,2,1:T(8,128)(2,1)} %bitcast.6), calls=%async_computation.2 | async-start | bytes 1572864 | tf_op jit(solution)/shard_map/all_to_all | solution.py:36
  670.1 955.5 %reduce-scatter.5.cloned.1.call-start = ((), (), s32[]{:S(2)}) async-start(), calls=%async_computation.10 | async-start | bytes 11796480 | tf_op jit(solution)/shard_map/reduce_scatter | solution.py:87
  723.9 52.9 %copy-start.2 = (bf16[128,4,768]{0,2,1:T(8,128)(2,1)}, bf16[128,4,768]{0,2,1:T(8,128)(2,1)S(1)}, u32[]{:S(2)}) copy-start(bf16[128,4,768]{0,2,1:T(8,128)(2,1)S(1)} %all-to-all-done.1) | copy-start | bytes 2359300
  825.8 4.7 copy-start.7
  825.8 109.2 %all-to-all-start = ((bf16[128,4,3072]{2,0,1:T(8,128)(2,1)}), bf16[128,4,3072]{2,0,1:T(8,128)(2,1)S(1)}, u32[]{:S(2)}, u32[]{:S(2)}) async-start(bf16[128,4,3072]{2,0,1:T(8,128)(2,1)} %bitcast.41), calls=%async_computation | async-start | bytes 6291456 | tf_op jit(solution)/shard_map/all_to_all | solution.py:47
  830.5 876.5 %reduce-scatter.3.cloned.1.call-start = ((), (), s32[]{:S(2)}) async-start(), calls=%async_computation.8 | async-start | bytes 11796480 | tf_op jit(solution)/shard_map/reduce_scatter | solution.py:75
  935.0 10.3 copy-start.1
  945.2 0.7 copy-start.8
  945.2 600.1 %copy-start = (bf16[128,12288]{1,0:T(8,128)(2,1)S(1)}, bf16[128,12288]{1,0:T(8,128)(2,1)}, u32[]{:S(2)}) copy-start(bf16[128,12288]{1,0:T(8,128)(2,1)} %all-gather.8.cloned.1.call-done) | copy-start | bytes 9437188
Sparse Core Ops, SparseCore 0:
  9.6 634.1 all-gather.5
  645.4 131.3 all-gather.13
  778.9 43.0 all-gather.7
  824.0 70.4 all-gather.11
  895.9 649.3 all-gather.9
  1548.4 77.2 reduce-scatter.4
  1628.8 78.1 reduce-scatter.2
where the time goes:
time: 1710 us
  waiting for transfers between devices  1430 us (84%)
  blocking collectives  174 us (10%)
  matrix products  67 us (4%)
    all_gather x1, waiting for transfers between devices, per_device(): lax.all_gather(second_weight, 'row', axis=1, tiled=True)  622 us
    all_gather x1, waiting for transfers between devices, per_device(): lax.all_gather(first_weight, 'row', axis=1, tiled=True)  596 us
    all_gather x1, blocking collectives, per_device(): lax.all_gather(input_scale.astype(jnp.bfloat16), 'row', axis=1, tiled=True)  101 us
    reduce_scatter x1, waiting for transfers between devices, per_device(): lax.psum_scatter(first_term.astype(jnp.bfloat16), 'depth', scatter_dimens...  81.4 us
    all_gather x1, blocking collectives, per_device(): lax.all_gather(hidden_scale.astype(jnp.bfloat16), 'row', axis=1, tiled=True)  53.5 us
    all_gather x1, waiting for transfers between devices, per_device(): lax.all_gather(hidden_stash, 'row', axis=0, tiled=True)  51.7 us
    reduce_scatter x1, waiting for transfers between devices, per_device(): lax.psum_scatter(second_term.astype(jnp.bfloat16), 'depth', scatter_dimen...  48 us
  transfers between devices with their start and end apart: 9, of which 6 were waited for; matrix products, arithmetic and copies ran while one was open for 5% of the time, Pallas kernels for 0%

commit v1 on v0

v1 whole, which is shorter than its diff:
```python
import jax
import jax.numpy as jnp
from jax import lax
from jax.sharding import PartitionSpec as P

root_two_over_pi = 0.7978845608028654
cubic_coef = 0.044715
contract_last = (((1,), (1,)), ((), ()))
contract_first = (((0,), (0,)), ((), ()))


def dequantize(values, scales):
    height = values.shape[0]
    breadth = values.shape[1]
    block = breadth // scales.shape[0]
    blocks = values.astype(jnp.float32).reshape(height, breadth // block, block)
    return (blocks * jnp.transpose(scales)[:, :, None]).reshape(height, breadth)


def gelu_value(before):
    tangent = jnp.tanh(root_two_over_pi * (before + cubic_coef * before * before * before))
    return 0.5 * before * (1.0 + tangent)


def gelu_slope(before):
    tangent = jnp.tanh(root_two_over_pi * (before + cubic_coef * before * before * before))
    return 0.5 * (1.0 + tangent) + 0.5 * before * (1.0 - tangent * tangent) * root_two_over_pi * (
        1.0 + 3.0 * cubic_coef * before * before
    )


def per_device(
    grad_out, input_stash, input_scale, hidden_stash, hidden_scale, first_weight, second_weight
):
    full_grad = lax.all_gather(grad_out, "col", axis=1, tiled=True)
    grad_rows = lax.all_to_all(full_grad, "row", split_axis=1, concat_axis=0, tiled=True)
    hidden_part = lax.dot_general(
        grad_rows, second_weight, contract_last, preferred_element_type=jnp.float32
    ).astype(jnp.bfloat16)
    hidden_grad = lax.psum_scatter(hidden_part, "row", scatter_dimension=0, tiled=True).astype(
        jnp.float32
    )
    before_gelu = dequantize(hidden_stash, hidden_scale)
    hidden_own = gelu_value(before_gelu).astype(jnp.bfloat16)
    gelu_grad = (hidden_grad * gelu_slope(before_gelu)).astype(jnp.bfloat16)
    full_gelu = lax.all_gather(gelu_grad, "col", axis=1, tiled=True)
    gelu_rows = lax.all_to_all(full_gelu, "row", split_axis=1, concat_axis=0, tiled=True)
    input_part = lax.dot_general(
        gelu_rows, first_weight, contract_last, preferred_element_type=jnp.float32
    ).astype(jnp.bfloat16)
    input_grad = lax.psum_scatter(input_part, "row", scatter_dimension=0, tiled=True)
    inputs_own = dequantize(input_stash, input_scale).astype(jnp.bfloat16)
    inputs = lax.all_gather(inputs_own, "row", axis=0, tiled=True)
    hidden = lax.all_gather(hidden_own, "row", axis=0, tiled=True)
    first_term = lax.dot_general(
        inputs, gelu_rows, contract_first, preferred_element_type=jnp.float32
    )
    first_column = jnp.sum(gelu_rows.astype(jnp.float32), axis=0)
    second_term = lax.dot_general(
        hidden, grad_rows, contract_first, preferred_element_type=jnp.float32
    )
    second_column = jnp.sum(grad_rows.astype(jnp.float32), axis=0)
    first_grad = lax.psum_scatter(
        first_term.astype(jnp.bfloat16), "depth", scatter_dimension=1, tiled=True
    )
    first_bias = lax.psum_scatter(
        first_column.astype(jnp.bfloat16), "depth", scatter_dimension=0, tiled=True
    ).astype(jnp.float32)
    second_grad = lax.psum_scatter(
        second_term.astype(jnp.bfloat16), "depth", scatter_dimension=1, tiled=True
    )
    second_bias = lax.psum_scatter(
        second_column.astype(jnp.bfloat16), "depth", scatter_dimension=0, tiled=True
    ).astype(jnp.float32)
    return input_grad, first_grad, first_bias, second_grad, second_bias


def solution(mesh):
    placed = (
        P(("row", "depth"), "col"),
        P(("row", "depth"), "col"),
        P("col", ("row", "depth")),
        P(("row", "depth"), "col"),
        P("col", ("row", "depth")),
        P("col", "row"),
        P("col", "row"),
    )
    return jax.shard_map(
        per_device,
        mesh=mesh,
        in_specs=placed,
        out_specs=(
            P(("row", "depth"), "col"),
            P("col", ("row", "depth")),
            P(("row", "depth")),
            P("col", ("row", "depth")),
            P(("row", "depth")),
        ),
        check_vma=False,
    )
```

time: 1710 us -> 627 us (0.37)
  waiting for transfers between devices: 1430 us -> 374 us
  matrix products: 67 us -> 39.6 us
    all_gather x4 -> x2, waiting for transfers between devices: 1270 us -> 45.1 us  [the longest x1 45.1 us: per_device(): hidden = lax.all_gather(hidden_own, 'row', axis=0, tiled=True)]
    all_to_all x0 -> x2, blocking collectives: none -> 162 us  [the longest x1 138 us: per_device(): lax.all_to_all(full_gelu, 'row', split_axis=1, concat_axis=0, tiled=True)]
    all_gather x2 -> x0, blocking collectives: 155 us -> none  [the longest x1 101 us: per_device(): lax.all_gather(input_scale.astype(jnp.bfloat16), 'row', axis=1, tiled=True)]
    reduce_scatter x0 -> x2, waiting for transfers between devices: none -> 122 us  [the longest x1 109 us: per_device(): lax.psum_scatter(hidden_part, 'row', scatter_dimension=0, tiled=True)]
    reduce_scatter x1, waiting for transfers between devices: 48 us -> 81.6 us  [per_device(): lax.psum_scatter(second_term.astype(jnp.bfloat16), 'depth', scatter_dimen...]
    dot_general x2, matrix products: 42 us -> 20 us  [the longest x1 11 us: per_device(): lax.dot_general(grad_rows, second_weight, contract_last, preferred_elemen...]
  transfers between devices with their start and end apart: 9 -> 7, of which waited for: 6 -> 6; matrix products, arithmetic and copies ran while one was open for 5% -> 6% of each run, Pallas kernels for 0% -> 0%
where the time goes in v1:
time: 627 us
  waiting for transfers between devices  374 us (60%)
  blocking collectives  182 us (29%)
  matrix products  39.6 us (6%)
  between operations  15.5 us (2%)
  other arithmetic  8.02 us (1%)
  local copies, waits for them, and re-layouts  7.23 us (1%)
    all_to_all x1, blocking collectives, per_device(): lax.all_to_all(full_gelu, 'row', split_axis=1, concat_axis=0, tiled=True)  138 us
    reduce_scatter x1, waiting for transfers between devices, per_device(): lax.psum_scatter(hidden_part, 'row', scatter_dimension=0, tiled=True)  109 us
    reduce_scatter x1, waiting for transfers between devices, per_device(): lax.psum_scatter(second_term.astype(jnp.bfloat16), 'depth', scatter_dimen...  81.6 us
    reduce_scatter x1, waiting for transfers between devices, per_device(): lax.psum_scatter(first_term.astype(jnp.bfloat16), 'depth', scatter_dimens...  80.5 us
    all_gather x1, waiting for transfers between devices, per_device(): hidden = lax.all_gather(hidden_own, 'row', axis=0, tiled=True)  45.1 us
    all_gather x1, waiting for transfers between devices, per_device(): full_gelu = lax.all_gather(gelu_grad, 'col', axis=1, tiled=True)  43.8 us
    all_to_all x1, blocking collectives, per_device(): lax.all_to_all(full_grad, 'row', split_axis=1, concat_axis=0, tiled=True)  24.1 us
    reduce_scatter x1, waiting for transfers between devices, per_device(): lax.psum_scatter(input_part, 'row', scatter_dimension=0, tiled=True)  12.8 us
  transfers between devices with their start and end apart: 7, of which 6 were waited for; matrix products, arithmetic and copies ran while one was open for 6% of the time, Pallas kernels for 0%

profile of v1, /device:TPU:0, one launch (start us, length us, event | category | flops | bytes accessed | tf_op | source)
XLA Modules:
  0.0 626.9 jit_solution(5742841960268730516)
XLA Ops:
  7.2 0.0 reduce-scatter.5.cloned.1.call-start
  7.2 1.2 copy.22
  8.4 12.7 %all_gather.12 = bf16[128,3072]{0,1:T(8,128)(2,1)S(1)} all-gather(bf16[128,1536]{0,1:T(8,128)(2,1)S(1)} %copy.22), channel_id=1, replica_groups=mesh['row'=4,'col'=2,'depth'=4] {'col'}, dimensions={1}, use_global_device_ids=true | all-gather | bytes 1179648 | tf_op jit(solution)/shard_map/all_gather | solution.py:35
  21.2 24.1 %all_to_all.38 = bf16[128,4,768]{0,2,1:T(8,128)(2,1)S(1)} all-to-all(bf16[128,4,768]{0,2,1:T(8,128)(2,1)S(1)} %bitcast.38), channel_id=1, replica_groups=mesh['row'=4,'col'=2,'depth'=4] {'row'}, dimensions={1} | all-to-all | bytes 1572864 | tf_op jit(solution)/shard_map/all_to_all | solution.py:36
  45.3 0.0 copy-start
  45.3 0.3 copy.23
  45.6 0.0 copy-start.3
  45.6 11.0 %convolution_convert_fusion.2 = bf16[512,6144]{1,0:T(8,128)(2,1)} fusion(bf16[512,768]{1,0:T(8,128)(2,1)S(1)} %bitcast.39, bf16[6144,768]{1,0:T(8,128)(2,1)} %param.13), kind=kOutput, calls=%fused_computation.2 | convolution fusion | flops 4834983936 | bytes 16515072 | tf_op jit(solution)/shard_map/dot_general | solution.py:37
  56.6 0.0 copy-done
  56.6 0.0 copy-done.3
  56.6 0.0 copy-start.5
  56.6 0.0 reduce-scatter.5.cloned.1.call-update
  56.6 0.0 copy-start.1
  56.6 0.0 all-gather.4.cloned.1.call-start
  56.7 0.6 copy-done.5
  57.3 0.1 copy.24
  57.4 109.2 %reduce-scatter.5.cloned.1.call-done = bf16[128,6144]{1,0:T(8,128)(2,1)} async-done(((bf16[512,6144]{1,0:T(8,128)(2,1)}), bf16[128,6144]{1,0:T(8,128)(2,1)}) %reduce-scatter.5.cloned.1.call-update) | async-done | bytes 1572880 | tf_op jit(solution)/shard_map/reduce_scatter | solution.py:40
  166.6 0.0 copy-start.2
  166.6 0.9 mul.72
  167.5 0.0 copy-done.1
  167.5 0.5 copy-done.2
  168.0 0.0 copy-start.4
  168.0 0.0 copy-start.6
  168.0 3.9 multiply_convert_fusion
  171.9 0.0 all-gather.4.cloned.1.call-update
  171.9 0.0 all-gather.6.cloned.1.call-start
  172.0 0.0 copy-done.4
  172.0 0.2 copy.26
  172.2 0.0 copy-done.6
  172.2 0.8 fusion.7
  173.1 0.0 all-gather.6.cloned.1.call-update
  173.1 0.0 all-gather.8.cloned.1.call-start
  173.1 0.5 all-gather.8.cloned.1.call-update
  173.7 0.0 reduce-scatter.7.cloned.1.call-start
  173.7 43.8 %all-gather.4.cloned.1.call-done = bf16[128,12288]{1,0:T(8,128)(2,1)} async-done(((bf16[128,6144]{1,0:T(8,128)(2,1)}), bf16[128,12288]{1,0:T(8,128)(2,1)}) %all-gather.4.cloned.1.call-update) | async-done | bytes 3145744 | tf_op jit(solution)/shard_map/all_gather | solution.py:46
  217.6 2.1 copy.35
  219.7 138.3 %all_to_all.39 = bf16[128,4,3072]{2,0,1:T(8,128)(2,1)S(1)} all-to-all(bf16[128,4,3072]{2,0,1:T(8,128)(2,1)S(1)} %bitcast.34), channel_id=1, replica_groups=mesh['row'=4,'col'=2,'depth'=4] {'row'}, dimensions={1} | all-to-all | bytes 6291456 | tf_op jit(solution)/shard_map/all_to_all | solution.py:47
  358.0 9.1 %convolution_convert_fusion.3 = bf16[512,1536]{1,0:T(8,128)(2,1)} fusion(bf16[512,3072]{1,0:T(8,128)(2,1)S(1)} %bitcast.32, bf16[1536,3072]{1,0:T(8,128)(2,1)} %param.12), kind=kOutput, calls=%fused_computation.15 | convolution fusion | flops 4832624640 | bytes 14155776 | tf_op jit(solution)/shard_map/dot_general | solution.py:48
  367.1 0.0 reduce-scatter.7.cloned.1.call-update
  367.1 0.0 reduce-scatter.9.cloned.1.call-start
  367.2 0.0 all-gather.6.cloned.1.call-done
  367.2 9.1 %convolution_convert_fusion = bf16[1536,3072]{1,0:T(8,128)(2,1)} fusion(bf16[512,1536]{0,1:T(8,128)(2,1)} %all-gather.6.cloned.1.call-done, bf16[512,3072]{1,0:T(8,128)(2,1)S(1)} %bitcast.33), kind=kOutput, calls=%fused_computation | convolution fusion | flops 4836556800 | bytes 14155776 | tf_op jit(solution)/shard_map/dot_general | solution.py:55
  376.3 0.0 reduce-scatter.9.cloned.1.call-update
  376.4 0.2 reduce-scatter.11.cloned.1.call-start
  376.6 45.1 %all-gather.8.cloned.1.call-done = bf16[512,6144]{1,0:T(8,128)(2,1)} async-done(((bf16[128,6144]{1,0:T(8,128)(2,1)}), bf16[512,6144]{1,0:T(8,128)(2,1)}) %all-gather.8.cloned.1.call-update) | async-done | bytes 6291472 | tf_op jit(solution)/shard_map/all_gather | solution.py:54
  421.7 10.4 %convolution_convert_fusion.1 = bf16[6144,768]{0,1:T(8,128)(2,1)} fusion(bf16[512,6144]{1,0:T(8,128)(2,1)} %all-gather.8.cloned.1.call-done, bf16[512,768]{1,0:T(8,128)(2,1)} %bitcast.40), kind=kOutput, calls=%fused_computation.1 | convolution fusion | flops 4836556800 | bytes 16515072 | tf_op jit(solution)/shard_map/dot_general | solution.py:59
  432.1 0.0 copy-start.7
  432.1 0.0 reduce-scatter.11.cloned.1.call-update
  432.1 0.6 copy-done.7
  432.8 0.6 dynamic-slice
  434.6 1.3 reduce_sum.25
  436.0 0.6 reduce_sum.24
  436.6 7.3 %all-reduce.2 = (bf16[3072]{0:T(1024)(128)(2,1)S(1)}, bf16[768]{0:T(1024)(128)(2,1)S(1)}) all-reduce(bf16[3072]{0:T(1024)(128)(2,1)S(1)} %reduce_sum.24, bf16[768]{0:T(1024)(128)(2,1)S(1)} %reduce_sum.25), channel_id=5, replica_groups=mesh['row'=4,'col'=2,'depth'=4] {'depth'}, use_global_device_ids=true, to_apply=%region_4.0.clone | all-reduce | flops 3840 | bytes 15360
  443.9 0.6 dynamic-slice_convert_fusion.1
  444.5 0.7 dynamic-slice_convert_fusion
  445.2 12.8 %reduce-scatter.7.cloned.1.call-done = bf16[128,1536]{1,0:T(8,128)(2,1)} async-done(((bf16[512,1536]{1,0:T(8,128)(2,1)}), bf16[128,1536]{1,0:T(8,128)(2,1)}) %reduce-scatter.7.cloned.1.call-update) | async-done | bytes 393232 | tf_op jit(solution)/shard_map/reduce_scatter | solution.py:51
  458.0 80.5 %reduce-scatter.9.cloned.1.call-done = bf16[1536,768]{1,0:T(8,128)(2,1)} async-done(((bf16[1536,3072]{1,0:T(8,128)(2,1)}), bf16[1536,768]{1,0:T(8,128)(2,1)}) %reduce-scatter.9.cloned.1.call-update) | async-done | bytes 2359312 | tf_op jit(solution)/shard_map/reduce_scatter | solution.py:63
  538.5 81.6 %reduce-scatter.11.cloned.1.call-done = bf16[6144,192]{0,1:T(8,128)(2,1)} async-done(((bf16[6144,768]{0,1:T(8,128)(2,1)}), bf16[6144,192]{0,1:T(8,128)(2,1)}) %reduce-scatter.11.cloned.1.call-update) | async-done | bytes 2359312 | tf_op jit(solution)/shard_map/reduce_scatter | solution.py:69
Async XLA Ops:
  7.2 159.4 %reduce-scatter.5.cloned.1.call-start = ((), (), s32[]{:S(2)}) async-start(), calls=%async_computation.6 | async-start | bytes 7864320 | tf_op jit(solution)/shard_map/reduce_scatter | solution.py:40
  45.3 11.3 %copy-start = (bf16[128,4,768]{0,2,1:T(8,128)(2,1)}, bf16[128,4,768]{0,2,1:T(8,128)(2,1)S(1)}, u32[]{:S(2)}) copy-start(bf16[128,4,768]{0,2,1:T(8,128)(2,1)S(1)} %all_to_all.38) | copy-start | bytes 2359300
  45.6 11.0 %copy-start.3 = (bf16[4,128,768]{2,1,0:T(8,128)(2,1)}, bf16[4,128,768]{2,1,0:T(8,128)(2,1)S(1)}, u32[]{:S(2)}) copy-start(bf16[4,128,768]{2,1,0:T(8,128)(2,1)S(1)} %copy.23) | copy-start | bytes 2359300
  56.6 0.7 copy-start.5
  56.6 110.9 %copy-start.1 = (bf16[128,6144]{1,0:T(8,128)(2,1)S(1)}, bf16[128,6144]{1,0:T(8,128)(2,1)}, u32[]{:S(2)}) copy-start(bf16[128,6144]{1,0:T(8,128)(2,1)} %param.10) | copy-start | bytes 4718596
  56.6 160.9 %all-gather.4.cloned.1.call-start = ((), (), s32[]{:S(2)}) async-start(), calls=%async_computation.7 | async-start | bytes 4718592 | tf_op jit(solution)/shard_map/all_gather | solution.py:46
  166.6 1.4 copy-start.2
  168.0 4.0 copy-start.4
  168.0 4.2 copy-start.6
  171.9 195.2 %all-gather.6.cloned.1.call-start = ((), (), s32[]{:S(2)}) async-start(), calls=%async_computation.9 | async-start | bytes 1966080 | tf_op jit(solution)/shard_map/all_gather | solution.py:53
  173.1 248.6 %all-gather.8.cloned.1.call-start = ((), (), s32[]{:S(2)}) async-start(), calls=%async_computation.11 | async-start | bytes 7864320 | tf_op jit(solution)/shard_map/all_gather | solution.py:54
  173.7 284.3 %reduce-scatter.7.cloned.1.call-start = ((), (), s32[]{:S(2)}) async-start(), calls=%async_computation.8 | async-start | bytes 1966080 | tf_op jit(solution)/shard_map/reduce_scatter | solution.py:51
  367.1 171.4 %reduce-scatter.9.cloned.1.call-start = ((), (), s32[]{:S(2)}) async-start(), calls=%async_computation.10 | async-start | bytes 11796480 | tf_op jit(solution)/shard_map/reduce_scatter | solution.py:63
  376.4 243.7 %reduce-scatter.11.cloned.1.call-start = ((), (), s32[]{:S(2)}) async-start(), calls=%async_computation.12 | async-start | bytes 11796480 | tf_op jit(solution)/shard_map/reduce_scatter | solution.py:69
  432.1 0.7 copy-start.7
Sparse Core Ops, SparseCore 0:
  56.7 109.8 reduce-scatter.4
  172.1 45.4 all-gather.3
  219.1 74.8 all-gather.5
  296.0 125.6 all-gather.7
  424.4 33.5 reduce-scatter.6
  461.0 77.4 reduce-scatter.8
  541.6 78.4 reduce-scatter.10
